TPU v7x, 32 devices: a whole 2x2x4 slice. The times are simulated.
32 devices in a mesh: rows: 8 (over y, x, core), cols: 4 (over z).
Axes of the slice: x: 2, y: 2, z: 4, core: 2. Of those that a mesh axis runs over, the one named last changes fastest.
Arguments:
- vectors: float32 [128, 81920], P('cols', 'rows'), may hold values from -6 to 6
- directions: float32 [128, 81920], P('cols', 'rows'), may hold values from -6 to 6
- tables: float32 [4, 640, 640], replicated, may hold values from -1 to 3
- counts: int32 [8], P('rows'), may hold values from 8 to 16, as said below
- send_lists: int32 [8, 2, 3], P('rows'), may hold values from 0 to 15, as said below
- neighbors: int32 [128, 7], P('rows'), may hold values from 0 to 21
- coupling_kinds: int32 [128, 7], P('rows'), may hold values from 0 to 3
- rotations: float32 [2, 384, 256], replicated, may hold values from -0.3125 to 0.3125
Outputs:
- new_vectors: float32 [128, 81920], P('cols', 'rows')
- new_directions: float32 [128, 81920], P('cols', 'rows')
Inputs may be any that keep to these rules, and one draw needn't show every extreme that they name: `counts`: at least one index of rows holds 16 live slots. `send_lists`: each list names 3 different live slots of its own index.
All inputs are finite; a program needn't handle non-finite values.
Results may differ from a plain program's by a relative error of at most 0.0003.
Values sent between devices are 32-bit elements; how exact they have to be, the bound alone decides.
A program may use at most 128 MiB of HBM per device.

v0:
```python
import jax
import jax.numpy as jnp
from jax import lax
from jax.sharding import PartitionSpec as P

highest = lax.Precision.HIGHEST


def shifted(array, axis, by):
    devices = lax.axis_size(axis)
    pairs = [(i, i + by) for i in range(devices) if 0 <= i + by < devices]
    return lax.ppermute(array, axis, pairs)


def apply_hamiltonian(vectors, tables, send_lists, neighbors, coupling_kinds):
    local_cols, length = vectors.shape
    slot_count = neighbors.shape[0]
    block_len = length // slot_count
    blocks = vectors.reshape(local_cols, slot_count, block_len).transpose(1, 0, 2)
    upward = blocks[send_lists[0, 1]]
    downward = blocks[send_lists[0, 0]]
    lower_ghosts = shifted(upward, "rows", 1)
    upper_ghosts = shifted(downward, "rows", -1)
    extended = jnp.concatenate([lower_ghosts, blocks, upper_ghosts], axis=0)
    picked = extended[neighbors]
    onehot = (coupling_kinds[:, :, None] == jnp.arange(tables.shape[0], dtype=jnp.int32)).astype(
        jnp.float32
    )
    grouped = jnp.einsum("cnt,cnkb->tckb", onehot, picked, precision=highest)
    result = jnp.einsum("tckb,tbe->cke", grouped, tables, precision=highest)
    return result.transpose(1, 0, 2).reshape(local_cols, length)


def factor_rotation(current, applied, previous, rotations_now, row_total, sum_small, sum_big):
    rayleigh = sum_small(jnp.dot(applied, current.T, precision=highest)) / row_total
    residual = applied - jnp.dot(rayleigh, current, precision=highest)
    stacked = jnp.concatenate([residual, current, previous], axis=0)
    gram_matrix = sum_big(jnp.dot(stacked, stacked.T, precision=highest)) / row_total
    factor = jnp.linalg.cholesky(gram_matrix)
    solved = lax.linalg.triangular_solve(
        factor, rotations_now, left_side=True, lower=True, transpose_a=True
    )
    return (stacked, solved)


def on_device(
    vectors, directions, tables, counts, send_lists, neighbors, coupling_kinds, rotations
):
    local_cols, length = vectors.shape
    slot_count = neighbors.shape[0]
    block_len = length // slot_count
    live_slots = (jnp.arange(slot_count, dtype=jnp.int32) < counts[0]).astype(jnp.float32)
    row_mask = jnp.repeat(live_slots, block_len)
    row_total = float(length * lax.axis_size("rows"))
    current = vectors * row_mask
    previous = directions * row_mask

    def sum_small(values):
        return lax.psum(values, ("rows", "cols"))

    def sum_big(values):
        return lax.psum(values, ("rows", "cols"))

    for iteration in range(rotations.shape[0]):
        applied = (
            apply_hamiltonian(current, tables, send_lists, neighbors, coupling_kinds) * row_mask
        )
        cur_part, app_part, prev_part = (
            lax.all_to_all(current, "cols", split_axis=1, concat_axis=0, tiled=True),
            lax.all_to_all(applied, "cols", split_axis=1, concat_axis=0, tiled=True),
            lax.all_to_all(previous, "cols", split_axis=1, concat_axis=0, tiled=True),
        )
        stacked, solved = factor_rotation(
            cur_part, app_part, prev_part, rotations[iteration], row_total, sum_small, sum_big
        )
        half_cols = solved.shape[1] // 2
        new_both = jnp.dot(solved.T, stacked, precision=highest)
        current, previous = (
            lax.all_to_all(new_both[:half_cols], "cols", split_axis=0, concat_axis=1, tiled=True),
            lax.all_to_all(new_both[half_cols:], "cols", split_axis=0, concat_axis=1, tiled=True),
        )
    return (current, previous)


def solution(mesh):
    return jax.shard_map(
        on_device,
        mesh=mesh,
        in_specs=(
            P("cols", "rows"),
            P("cols", "rows"),
            P(),
            P("rows"),
            P("rows", None, None),
            P("rows", None),
            P("rows", None),
            P(),
        ),
        out_specs=(P("cols", "rows"), P("cols", "rows")),
        check_vma=False,
    )
```

profile of v0, /device:TPU:0, one launch (start us, length us, event | category | flops | bytes accessed | tf_op | source)
XLA Modules:
  0.0 1102.0 jit_solution(264226218503280197)
XLA Ops:
  35.1 13.5 %fusion.14 = f32[4,16,32,640]{3,0,2,1:T(4,128)S(1)} fusion(f32[16,7,32,640]{3,2,1,0:T(8,128)} %bitcast.188, s32[16,7]{1,0:T(8,128)S(1)} %copy.61), kind=kOutput, calls=%fused_computation.28 | convolution fusion | flops 110100928 | bytes 14418368 | tf_op jit(solution)/shard_map/cnt,cnkb->tckb/dot_general | solution.py:29
  48.6 15.4 %fusion.20 = f32[32,16,640]{2,0,1:T(8,128)S(1)} fusion(f32[4,640,640]{2,1,0:T(8,128)} %param.13, f32[4,16,32,640]{3,0,2,1:T(4,128)S(1)} %fusion.14), kind=kOutput, calls=%fused_computation.32 | convolution fusion | flops 10066329600 | bytes 13107200 | tf_op jit(solution)/shard_map/tckb,tbe->cke/dot_general | solution.py:30
  76.8 29.2 %all-to-all-done = f32[32,4,2560]{2,0,1:T(8,128)S(1)} async-done(((f32[32,4,2560]{2,0,1:T(8,128)}), f32[32,4,2560]{2,0,1:T(8,128)S(1)}, u32[]{:S(2)}, u32[]{:S(2)}) %all-to-all-start) | async-done | bytes 1310752 | tf_op jit(solution)/shard_map/all_to_all | solution.py:70
  112.3 132.5 %all-reduce.6.cloned.1.call-done = f32[128,128]{1,0:T(8,128)} async-done(((f32[128,128]{1,0:T(8,128)}), f32[128,128]{1,0:T(8,128)}) %all-reduce.6.cloned.1.call-update) | async-done | bytes 65552 | tf_op jit(solution)/shard_map/psum | solution.py:59
  258.9 127.2 %all-reduce.8.cloned.1.call-done = f32[384,384]{0,1:T(8,128)} async-done(((f32[384,384]{0,1:T(8,128)}), f32[384,384]{0,1:T(8,128)}) %all-reduce.8.cloned.1.call-update) | async-done | bytes 589840 | tf_op jit(solution)/shard_map/psum | solution.py:62
  387.6 11.7 %cholesky.208 = f32[128,128]{1,0:T(8,128)S(1)} custom-call(f32[128,128]{1,0:T(8,128)S(1)} %cholesky.310), custom_call_target="Cholesky" | custom-call | tf_op jit(solution)/shard_map/jit(cholesky)/cholesky | solution.py:39
  409.8 11.7 %cholesky.227 = f32[128,128]{1,0:T(8,128)S(1)} custom-call(f32[128,128]{1,0:T(8,128)S(1)} %cholesky.314), custom_call_target="Cholesky" | custom-call | tf_op jit(solution)/shard_map/jit(cholesky)/cholesky | solution.py:39
  421.5 10.0 custom-call.21
  432.0 11.7 %cholesky.246 = f32[128,128]{1,0:T(8,128)S(1)} custom-call(f32[128,128]{1,0:T(8,128)S(1)} %convolution_subtract_fusion.9), custom_call_target="Cholesky" | custom-call | tf_op jit(solution)/shard_map/jit(cholesky)/cholesky | solution.py:39
  454.0 30.7 %custom-call.22 = f32[3,128,128]{1,2,0:T(8,128)S(1)} custom-call(f32[3,128,128]{2,1,0:T(8,128)} %copy-done.6), custom_call_target="InvertDiagBlocksLowerTriangular" | custom-call | tf_op jit(solution)/shard_map/triangular_solve/custom-call.2 | solution.py:40
  496.0 35.2 %all_to_all.172 = f32[4,32,2560]{2,1,0:T(8,128)} all-to-all(f32[4,32,2560]{2,1,0:T(8,128)S(1)} %bitcast.210), channel_id=1, replica_groups=mesh['rows'=8,'cols'=4] {'cols'}, dimensions={0} | all-to-all | bytes 2621440 | tf_op jit(solution)/shard_map/all_to_all | solution.py:79
  550.3 15.8 %all-to-all-done.6 = f32[4,32,2560]{2,1,0:T(8,128)} async-done(((f32[4,32,2560]{2,1,0:T(8,128)}), f32[4,32,2560]{2,1,0:T(8,128)}, u32[]{:S(2)}, u32[]{:S(2)}) %all-to-all-start.6) | async-done | bytes 1310752 | tf_op jit(solution)/shard_map/all_to_all | solution.py:80
  569.8 13.5 %fusion.17 = f32[4,16,32,640]{3,0,2,1:T(4,128)S(1)} fusion(f32[16,7,32,640]{3,2,1,0:T(8,128)} %bitcast.187, s32[16,7]{1,0:T(8,128)S(1)} %copy.61), kind=kOutput, calls=%fused_computation.29 | convolution fusion | flops 110100928 | bytes 14418368 | tf_op jit(solution)/shard_map/cnt,cnkb->tckb/dot_general | solution.py:29
  583.3 15.4 %fusion.25 = f32[32,16,640]{2,0,1:T(8,128)S(1)} fusion(f32[4,640,640]{2,1,0:T(8,128)} %param.13, f32[4,16,32,640]{3,0,2,1:T(4,128)S(1)} %fusion.17), kind=kOutput, calls=%fused_computation.33 | convolution fusion | flops 10066329600 | bytes 13107200 | tf_op jit(solution)/shard_map/tckb,tbe->cke/dot_general | solution.py:30
  603.9 35.3 %all_to_all.173 = f32[32,4,2560]{2,0,1:T(8,128)S(1)} all-to-all(f32[32,4,2560]{2,0,1:T(8,128)} %copy.75), channel_id=1, replica_groups=mesh['rows'=8,'cols'=4] {'cols'}, dimensions={1} | all-to-all | bytes 2621440 | tf_op jit(solution)/shard_map/all_to_all | solution.py:70
  645.5 128.5 %all-reduce.10.cloned.1.call-done = f32[128,128]{1,0:T(8,128)} async-done(((f32[128,128]{1,0:T(8,128)}), f32[128,128]{1,0:T(8,128)}) %all-reduce.10.cloned.1.call-update) | async-done | bytes 65552 | tf_op jit(solution)/shard_map/psum | solution.py:59
  787.0 128.2 %all-reduce.12.cloned.1.call-done = f32[384,384]{0,1:T(8,128)} async-done(((f32[384,384]{0,1:T(8,128)}), f32[384,384]{0,1:T(8,128)}) %all-reduce.12.cloned.1.call-update) | async-done | bytes 589840 | tf_op jit(solution)/shard_map/psum | solution.py:62
  916.8 11.7 %cholesky.261 = f32[128,128]{1,0:T(8,128)S(1)} custom-call(f32[128,128]{1,0:T(8,128)S(1)} %cholesky.318), custom_call_target="Cholesky" | custom-call | tf_op jit(solution)/shard_map/jit(cholesky)/cholesky | solution.py:39
  939.0 11.7 %cholesky.280 = f32[128,128]{1,0:T(8,128)S(1)} custom-call(f32[128,128]{1,0:T(8,128)S(1)} %cholesky.322), custom_call_target="Cholesky" | custom-call | tf_op jit(solution)/shard_map/jit(cholesky)/cholesky | solution.py:39
  950.8 10.0 custom-call.24
  961.2 11.7 %cholesky.299 = f32[128,128]{1,0:T(8,128)S(1)} custom-call(f32[128,128]{1,0:T(8,128)S(1)} %convolution_subtract_fusion.8), custom_call_target="Cholesky" | custom-call | tf_op jit(solution)/shard_map/jit(cholesky)/cholesky | solution.py:39
  983.8 30.6 %custom-call.25 = f32[3,128,128]{1,2,0:T(8,128)S(1)} custom-call(f32[3,128,128]{2,1,0:T(8,128)} %copy-done.5), custom_call_target="InvertDiagBlocksLowerTriangular" | custom-call | tf_op jit(solution)/shard_map/triangular_solve/custom-call.2 | solution.py:40
  1025.7 34.5 %all_to_all.174 = f32[4,32,2560]{2,1,0:T(8,128)S(1)} all-to-all(f32[4,32,2560]{2,1,0:T(8,128)S(1)} %bitcast.211), channel_id=1, replica_groups=mesh['rows'=8,'cols'=4] {'cols'}, dimensions={0} | all-to-all | bytes 2621440 | tf_op jit(solution)/shard_map/all_to_all | solution.py:79
  1064.9 29.0 %all-to-all-done.9 = f32[4,32,2560]{2,1,0:T(8,128)S(1)} async-done(((f32[4,32,2560]{2,1,0:T(8,128)}), f32[4,32,2560]{2,1,0:T(8,128)S(1)}, u32[]{:S(2)}, u32[]{:S(2)}) %all-to-all-start.9) | async-done | bytes 1310752 | tf_op jit(solution)/shard_map/all_to_all | solution.py:80
  (168 shorter events, 189.9 us)
Async XLA Ops:
  12.0 57.2 %all-to-all-start.1 = ((f32[32,4,2560]{2,0,1:T(8,128)}), f32[32,4,2560]{2,0,1:T(8,128)S(1)}, u32[]{:S(2)}, u32[]{:S(2)}) async-start(f32[32,4,2560]{2,0,1:T(8,128)} %bitcast.212), calls=%async_computation.1 | async-start | bytes 2621440 | tf_op jit(solution)/shard_map/all_to_all | solution.py:69
  18.3 1.2 copy-start.9
  18.3 10.1 copy-start.8
  18.3 10.3 copy-start.7
  21.5 7.3 collective-permute-start.1
  24.7 4.3 collective-permute-start
  69.2 36.8 %all-to-all-start = ((f32[32,4,2560]{2,0,1:T(8,128)}), f32[32,4,2560]{2,0,1:T(8,128)S(1)}, u32[]{:S(2)}, u32[]{:S(2)}) async-start(f32[32,4,2560]{2,0,1:T(8,128)} %copy.65), calls=%async_computation | async-start | bytes 2621440 | tf_op jit(solution)/shard_map/all_to_all | solution.py:70
  106.0 141.9 %all-to-all-start.2 = ((f32[32,4,2560]{2,0,1:T(8,128)}), f32[32,4,2560]{2,0,1:T(8,128)}, u32[]{:S(2)}, u32[]{:S(2)}) async-start(f32[32,4,2560]{2,0,1:T(8,128)} %bitcast.213), calls=%async_computation.2 | async-start | bytes 2621440 | tf_op jit(solution)/shard_map/all_to_all | solution.py:71
  110.3 134.5 %all-reduce.6.cloned.1.call-start = ((), (), s32[]{:S(2)}) async-start(), calls=%async_computation.10 | async-start | bytes 131072 | tf_op jit(solution)/shard_map/psum | solution.py:59
  112.2 273.9 %all-reduce.8.cloned.1.call-start = ((), (), s32[]{:S(2)}) async-start(), calls=%async_computation.11 | async-start | bytes 1179648 | tf_op jit(solution)/shard_map/psum | solution.py:62
  247.9 10.0 copy-start.4
  386.1 1.4 copy-start.2
  447.2 41.7 %copy-start = (f32[128,2560]{1,0:T(8,128)S(1)}, f32[128,2560]{1,0:T(8,128)}, u32[]{:S(2)}) copy-start(f32[128,2560]{1,0:T(8,128)} %convolution_subtract_fusion.1) | copy-start | bytes 3932164
  453.3 0.7 copy-start.6
  531.3 34.8 %all-to-all-start.6 = ((f32[4,32,2560]{2,1,0:T(8,128)}), f32[4,32,2560]{2,1,0:T(8,128)}, u32[]{:S(2)}, u32[]{:S(2)}) async-start(f32[4,32,2560]{2,1,0:T(8,128)} %bitcast.43), calls=%async_computation.6 | async-start | bytes 2621440 | tf_op jit(solution)/shard_map/all_to_all | solution.py:80
  540.0 4.4 collective-permute-start.3
  541.3 4.2 collective-permute-start.2
  566.1 37.8 %all-to-all-start.5 = ((f32[32,4,2560]{2,0,1:T(8,128)}), f32[32,4,2560]{2,0,1:T(8,128)S(1)}, u32[]{:S(2)}, u32[]{:S(2)}) async-start(f32[32,4,2560]{2,0,1:T(8,128)} %bitcast.31), calls=%async_computation.5 | async-start | bytes 2621440 | tf_op jit(solution)/shard_map/all_to_all | solution.py:69
  639.2 137.9 %all-to-all-start.7 = ((f32[32,4,2560]{2,0,1:T(8,128)}), f32[32,4,2560]{2,0,1:T(8,128)}, u32[]{:S(2)}, u32[]{:S(2)}) async-start(f32[32,4,2560]{2,0,1:T(8,128)} %bitcast.44), calls=%async_computation.7 | async-start | bytes 2621440 | tf_op jit(solution)/shard_map/all_to_all | solution.py:71
  643.5 130.4 %all-reduce.10.cloned.1.call-start = ((), (), s32[]{:S(2)}) async-start(), calls=%async_computation.12 | async-start | bytes 131072 | tf_op jit(solution)/shard_map/psum | solution.py:59
  645.4 269.9 %all-reduce.12.cloned.1.call-start = ((), (), s32[]{:S(2)}) async-start(), calls=%async_computation.13 | async-start | bytes 1179648 | tf_op jit(solution)/shard_map/psum | solution.py:62
  915.3 1.4 copy-start.3
  977.0 41.6 %copy-start.1 = (f32[128,2560]{1,0:T(8,128)S(1)}, f32[128,2560]{1,0:T(8,128)}, u32[]{:S(2)}) copy-start(f32[128,2560]{1,0:T(8,128)} %convolution_subtract_fusion) | copy-start | bytes 3932164
  1060.2 33.7 %all-to-all-start.9 = ((f32[4,32,2560]{2,1,0:T(8,128)}), f32[4,32,2560]{2,1,0:T(8,128)S(1)}, u32[]{:S(2)}, u32[]{:S(2)}) async-start(f32[4,32,2560]{2,1,0:T(8,128)} %bitcast.58), calls=%async_computation.9 | async-start | bytes 2621440 | tf_op jit(solution)/shard_map/all_to_all | solution.py:80
  (1 other events, 0.7 us)
Sparse Core Ops, SparseCore 0:
  117.3 127.4 all-reduce.5
  258.0 128.0 all-reduce.7
  651.4 122.4 all-reduce.9
  787.2 128.0 all-reduce.11
where the time goes:
time: 1110 us; the launch traced here: 1100 us
  waiting for transfers between devices  592 us (53%)
  other arithmetic  182 us (16%)
  matrix products  110 us (10%)
  blocking collectives  105 us (9%)
  local copies, waits for them, and re-layouts  52.6 us (5%)
  starting transfers between devices  41.1 us (4%)
  between operations  19.4 us (2%)
    psum x2, waiting for transfers between devices, sum_small(): return lax.psum(values, ('rows', 'cols'))  261 us
    psum x2, waiting for transfers between devices, sum_big(): return lax.psum(values, ('rows', 'cols'))  255 us
    another operation x21, other arithmetic, factor_rotation(): factor = jnp.linalg.cholesky(gram_matrix)  113 us
    all_to_all x2, blocking collectives, on_device(): lax.all_to_all(new_both[:half_cols], 'cols', split_axis=0, concat_axis=1,...  69.7 us
    another operation x5, other arithmetic, factor_rotation(): lax.linalg.triangular_solve(factor, rotations_now, left_side=True, lower=...  61.4 us
    all_to_all x2, waiting for transfers between devices, on_device(): lax.all_to_all(new_both[half_cols:], 'cols', split_axis=0, concat_axis=1,...  44.8 us
    all_to_all x1, blocking collectives, on_device(): lax.all_to_all(applied, 'cols', split_axis=1, concat_axis=0, tiled=True)  35.3 us
    dot_general x2, matrix products, apply_hamiltonian(): result = jnp.einsum('tckb,tbe->cke', grouped, tables, precision=highest)  30.8 us
  transfers between devices with their start and end apart: 15, of which 9 were waited for; matrix products, arithmetic and copies ran while one was open for 9% of the time, Pallas kernels for 0%

commit v1 on v0

v1 whole, which is shorter than its diff:
```python
import functools
import jax
import jax.numpy as jnp
from jax import lax
from jax.experimental import pallas as pl
from jax.experimental.pallas import tpu as pltpu
from jax.sharding import PartitionSpec as P

highest = lax.Precision.HIGHEST
high = lax.Precision.HIGH
AXES = ("rows", "cols")


def shifted(array, axis, by):
    devices = lax.axis_size(axis)
    pairs = [(i, i + by) for i in range(devices) if 0 <= i + by < devices]
    return lax.ppermute(array, axis, pairs)


def split_parts(array):
    top = lax.reduce_precision(array, 8, 7)
    return top.astype(jnp.bfloat16), (array - top).astype(jnp.bfloat16)


def hamiltonian_kernel(group, counts, near, kinds, ext, top_ref, low_ref, out_ref, sums):
    types, depth, cols = sums.shape[0], sums.shape[2], out_ref.shape[1]
    step = pl.program_id(0)
    sums[...] = jnp.zeros_like(sums)
    for s in range(group):
        slot = step * group + s
        for j in range(near.shape[1]):
            where = kinds[slot, j]
            rows = pl.ds(s * cols, cols)
            sums[where, rows, :] = sums[where, rows, :] + ext[near[slot, j]]
    total = jnp.zeros((group * cols, depth), jnp.float32)
    for t in range(types):
        value = sums[t]
        top = value.astype(jnp.bfloat16)
        low = (value - top.astype(jnp.float32)).astype(jnp.bfloat16)
        dot = functools.partial(jnp.dot, preferred_element_type=jnp.float32)
        total += dot(top, top_ref[t]) + (dot(low, top_ref[t]) + dot(top, low_ref[t]))
    for s in range(group):
        live = ((step * group + s) < counts[0]).astype(jnp.float32)
        out_ref[s] = total[s * cols : (s + 1) * cols] * live


def apply_hamiltonian(blocks, tables_top, tables_low, counts, send_lists, neighbors, kinds):
    slots, cols, depth = blocks.shape
    types = tables_top.shape[0]
    lower = shifted(blocks[send_lists[0, 1]], "rows", 1)
    upper = shifted(blocks[send_lists[0, 0]], "rows", -1)
    extended = jnp.concatenate([lower, blocks, upper], axis=0)
    group = 4
    whole = lambda shape: pl.BlockSpec(shape, lambda i: (0,) * len(shape))
    smem = pl.BlockSpec(memory_space=pltpu.SMEM)
    return pl.pallas_call(
        functools.partial(hamiltonian_kernel, group),
        grid=(slots // group,),
        out_shape=jax.ShapeDtypeStruct(blocks.shape, jnp.float32),
        in_specs=[
            smem,
            smem,
            smem,
            whole(extended.shape),
            whole(tables_top.shape),
            whole(tables_low.shape),
        ],
        out_specs=pl.BlockSpec((group, cols, depth), lambda i: (i, 0, 0)),
        scratch_shapes=[pltpu.VMEM((types, group * cols, depth), jnp.float32)],
        compiler_params=pltpu.CompilerParams(vmem_limit_bytes=48 * 2**20),
        cost_estimate=pl.CostEstimate(
            flops=6 * types * slots * cols * depth * depth,
            bytes_accessed=4 * (extended.size + tables_top.size + blocks.size),
            transcendentals=0,
        ),
    )(counts, neighbors, kinds, extended, tables_top, tables_low)


def dot_nn(a, b):
    return jnp.dot(a, b, precision=highest, preferred_element_type=jnp.float32)


def dot_nt(a, b):
    return lax.dot_general(
        a, b, (((1,), (1,)), ((), ())), precision=highest, preferred_element_type=jnp.float32
    )


def dot_tn(a, b):
    return lax.dot_general(
        a, b, (((0,), (0,)), ((), ())), precision=highest, preferred_element_type=jnp.float32
    )


def inverse_factor(a):
    n = a.shape[0]
    ids = lax.broadcasted_iota(jnp.int32, (n, n), 0)
    lanes = lax.broadcasted_iota(jnp.int32, (n, n), 1)
    row_ids = lax.broadcasted_iota(jnp.int32, (n, 1), 0)
    eye = (ids == lanes).astype(jnp.float32)
    a_rows = [a[r : r + 8] for r in range(0, n, 8)]
    i_rows = [eye[r : r + 8] for r in range(0, n, 8)]
    for k in range(n - 1):
        g, r = k // 8, k % 8
        row_a, row_i = a_rows[g][r : r + 1], i_rows[g][r : r + 1]
        inv = 1.0 / row_a[:, k : k + 1]
        row_a, row_i = row_a * inv, row_i * inv
        for h in range(g, n // 8):
            factor = a_rows[h][:, k : k + 1]
            if h == g:
                factor = jnp.where(row_ids[g * 8 : g * 8 + 8] > k, factor, 0.0)
            a_rows[h] = a_rows[h] - factor * row_a
            i_rows[h] = i_rows[h] - factor * row_i
    a = jnp.concatenate(a_rows, axis=0)
    inverse = jnp.concatenate(i_rows, axis=0)
    pivots = jnp.sum(jnp.where(ids == lanes, a, 0.0), axis=1, keepdims=True)
    return inverse * lax.rsqrt(pivots)


def chain_kernel(gram_ref, rot_ref, out_ref, work, inv_ref, coef, mixed):
    k = gram_ref.shape[0] // 5
    at = lambda i: slice(i * k, (i + 1) * k)
    three = work.shape[0] // k

    def solve(iteration):
        rayleigh = work[at(0), at(1)]
        changed = work[at(0), :] - dot_nn(rayleigh, work[at(1), :])
        corner = changed[:, at(0)] - dot_nt(changed[:, at(1)], rayleigh)
        work[at(0), at(0)] = corner
        for i in (1, 2):
            work[at(i), at(0)] = changed[:, at(i)].T

        def block(b, carry):
            here = pl.ds(pl.multiple_of(b * k, k), k)
            inv_ref[here, :] = inverse_factor(work[here, here])
            return carry

        for b in range(three):
            block(b, 0)
            inverse = inv_ref[at(b), :]
            panels = [dot_nt(work[at(i), at(b)], inverse) for i in range(b + 1, three)]
            for i in range(b + 1, three):
                work[at(i), at(b)] = panels[i - b - 1]
                for j in range(b + 1, i + 1):
                    work[at(i), at(j)] = work[at(i), at(j)] - dot_nt(
                        panels[i - b - 1], panels[j - b - 1]
                    )
        parts = [None] * three
        for b in reversed(range(three)):
            value = rot_ref[iteration, at(b), :]
            for i in range(b + 1, three):
                value = value - dot_tn(work[at(i), at(b)], parts[i])
            parts[b] = dot_tn(inv_ref[at(b), :], value)
        coef[at(0), :] = parts[0]
        coef[at(1), :] = parts[1] - dot_tn(rayleigh, parts[0])
        coef[at(2), :] = parts[2]

    order = (2, 0, 1)
    for i in range(3):
        for j in range(3):
            work[at(i), at(j)] = gram_ref[at(order[i]), at(order[j])]
    solve(0)
    mixed[...] = jnp.zeros_like(mixed)
    for source, plain, applied in ((0, 2, 4), (1, 0, 2), (2, 1, 3)):
        first = coef[at(source), at(0)]
        mixed[at(applied), at(0)] = first
        mixed[at(plain), at(1)] = first
        mixed[at(plain), at(2)] = coef[at(source), at(1)]
    work[...] = dot_tn(mixed[...], dot_nn(gram_ref[...], mixed[...]))
    solve(1)
    out_ref[...] = dot_nn(mixed[...], coef[...])


def rotation_chain(gram, rotations):
    size = gram.shape[0]
    k = size // 5
    return pl.pallas_call(
        chain_kernel,
        out_shape=jax.ShapeDtypeStruct((size, 2 * k), jnp.float32),
        in_specs=[pl.BlockSpec(memory_space=pltpu.VMEM)] * 2,
        out_specs=pl.BlockSpec(memory_space=pltpu.VMEM),
        scratch_shapes=[
            pltpu.VMEM((3 * k, 3 * k), jnp.float32),
            pltpu.VMEM((3 * k, k), jnp.float32),
            pltpu.VMEM((3 * k, 2 * k), jnp.float32),
            pltpu.VMEM((size, 3 * k), jnp.float32),
        ],
        compiler_params=pltpu.CompilerParams(vmem_limit_bytes=48 * 2**20),
    )(gram, rotations)


def summed(values):
    rows, cols = lax.axis_size("rows"), lax.axis_size("cols")
    shape = values.shape
    swap = functools.partial(lax.all_to_all, split_axis=0, concat_axis=0, tiled=True)
    parts = values.reshape(rows, cols, -1)
    part = jnp.sum(swap(parts, "rows"), axis=0)
    part = jnp.sum(swap(part, "cols"), axis=0)
    line = swap(jnp.broadcast_to(part, (cols,) + part.shape), "cols")
    return swap(jnp.broadcast_to(line, (rows,) + line.shape), "rows").reshape(shape)


def on_device(
    vectors, directions, tables, counts, send_lists, neighbors, coupling_kinds, rotations
):
    local, length = vectors.shape
    slots = neighbors.shape[0]
    depth = length // slots
    cols = lax.axis_size("cols")
    k = local * cols
    row_total = float(length * lax.axis_size("rows"))
    live = (jnp.arange(slots, dtype=jnp.int32) < counts[0]).astype(jnp.float32)
    both = jnp.concatenate([vectors, directions], axis=0).reshape(2 * local, slots, depth)
    both = both.transpose(1, 0, 2) * live[:, None, None]
    top, low = split_parts(tables)
    apply = functools.partial(
        apply_hamiltonian,
        tables_top=top,
        tables_low=low,
        counts=counts,
        send_lists=send_lists,
        neighbors=neighbors,
        kinds=coupling_kinds,
    )

    def to_rows(blocks):
        swapped = lax.all_to_all(blocks, "cols", split_axis=0, concat_axis=0, tiled=True)
        count = blocks.shape[1] // local
        swapped = swapped.reshape(cols, slots // cols, count, local, depth)
        return swapped.transpose(2, 0, 3, 1, 4).reshape(count * k, length // cols)

    both_rows = to_rows(both)
    applied = apply(both)
    applied_rows = to_rows(applied)
    twice = apply(applied[:, :local])
    basis = jnp.concatenate([both_rows, applied_rows, to_rows(twice)], axis=0)
    gram = jnp.dot(basis, basis.T, precision=high)
    pairs = [(i, j) for i in range(5) for j in range(i + 1)]
    at = lambda i: slice(i * k, (i + 1) * k)
    packed = summed(jnp.concatenate([gram[at(i), at(j)] for i, j in pairs], axis=0)) / row_total
    tiles = {pair: packed[at(n)] for n, pair in enumerate(pairs)}
    gram = jnp.concatenate(
        [
            jnp.concatenate(
                [tiles[i, j] if i >= j else tiles[j, i].T for j in range(5)], axis=1
            )
            for i in range(5)
        ],
        axis=0,
    )
    mix = rotation_chain(gram, rotations)

    def finish(part):
        made = lax.dot_general(part, basis, (((0,), (0,)), ((), ())), precision=high)
        return lax.all_to_all(made, "cols", split_axis=0, concat_axis=1, tiled=True)

    return (finish(mix[:, :k]), finish(mix[:, k:]))


def solution(mesh):
    return jax.shard_map(
        on_device,
        mesh=mesh,
        in_specs=(
            P("cols", "rows"),
            P("cols", "rows"),
            P(),
            P("rows"),
            P("rows", None, None),
            P("rows", None),
            P("rows", None),
            P(),
        ),
        out_specs=(P("cols", "rows"), P("cols", "rows")),
        check_vma=False,
    )
```

time: 1110 us -> 484 us (0.44)
  waiting for transfers between devices: 592 us -> 109 us
  other arithmetic: 182 us -> 14.5 us
  Pallas kernels: 0 us -> 114 us
  matrix products: 110 us -> 20.8 us
  blocking collectives: 105 us -> 154 us
  between operations: 19.4 us -> 2.13 us
  starting transfers between devices: 41.1 us -> 24.3 us
  local copies, waits for them, and re-layouts: 52.6 us -> 38.3 us
    psum x4 -> x0, waiting for transfers between devices: 516 us -> none  [the longest x2 261 us: sum_small(): return lax.psum(values, ('rows', 'cols'))]
    another operation x26 -> x0, other arithmetic: 175 us -> none  [the longest x21 113 us: factor_rotation(): factor = jnp.linalg.cholesky(gram_matrix)]
    pallas_call x0 -> x3, Pallas kernels: none -> 114 us  [the longest x1 79.9 us: rotation_chain(): pl.pallas_call(chain_kernel, out_shape=jax.ShapeDtypeStruct((size, 2 * k)...]
    dot_general x12 -> x3, matrix products: 99.4 us -> 20.8 us  [the longest x2 12.3 us: finish(): lax.dot_general(part, basis, (((0,), (0,)), ((), ())), precision=high)]
    all_to_all x3 -> x6, blocking collectives: 105 us -> 154 us  [the longest x2 99.5 us: to_rows(): lax.all_to_all(blocks, 'cols', split_axis=0, concat_axis=0, tiled=True)]
    all_to_all x7 -> x3, waiting for transfers between devices: 74.1 us -> 107 us  [the longest x2 54.9 us: finish(): return lax.all_to_all(made, 'cols', split_axis=0, concat_axis=1, tiled=True)]
    all_to_all x7 -> x3, starting transfers between devices: 31.6 us -> 11.3 us  [the longest x2 7.08 us: finish(): return lax.all_to_all(made, 'cols', split_axis=0, concat_axis=1, tiled=True)]
    unnamed x25 -> x68, local copies, waits for them, and re-layouts: 1.58 us -> 16.9 us
  transfers between devices with their start and end apart: 15 -> 7, of which waited for: 9 -> 4; matrix products, arithmetic and copies ran while one was open for 9% -> 4% of each run, Pallas kernels for 0% -> 0%
where the time goes in v1:
time: 484 us; the launch traced here: 476 us
  blocking collectives  154 us (32%)
  Pallas kernels  114 us (24%)
  waiting for transfers between devices  109 us (23%)
  local copies, waits for them, and re-layouts  38.3 us (8%)
  starting transfers between devices  24.3 us (5%)
  matrix products  20.8 us (4%)
  other arithmetic  14.5 us (3%)
    all_to_all x2, blocking collectives, to_rows(): lax.all_to_all(blocks, 'cols', split_axis=0, concat_axis=0, tiled=True)  99.5 us
    pallas_call x1, Pallas kernels, rotation_chain(): pl.pallas_call(chain_kernel, out_shape=jax.ShapeDtypeStruct((size, 2 * k)...  79.9 us
    all_to_all x2, waiting for transfers between devices, finish(): return lax.all_to_all(made, 'cols', split_axis=0, concat_axis=1, tiled=True)  54.9 us
    all_to_all x1, waiting for transfers between devices, to_rows(): lax.all_to_all(blocks, 'cols', split_axis=0, concat_axis=0, tiled=True)  51.7 us
    pallas_call x2, Pallas kernels, apply_hamiltonian(): pl.pallas_call(functools.partial(hamiltonian_kernel, group), grid=(slots...  33.6 us
    all_to_all x1, blocking collectives, summed(): part = jnp.sum(swap(parts, 'rows'), axis=0)  20.5 us
    all_to_all x1, blocking collectives, summed(): swap(jnp.broadcast_to(line, (rows,) + line.shape), 'rows').reshape(shape)  17.1 us
    unnamed x68, local copies, waits for them, and re-layouts  16.9 us
  transfers between devices with their start and end apart: 7, of which 4 were waited for; matrix products, arithmetic and copies ran while one was open for 4% of the time, Pallas kernels for 0%

profile of v1, /device:TPU:0, one launch (start us, length us, event | category | flops | bytes accessed | tf_op | source)
XLA Modules:
  0.0 476.1 jit_solution(12175525164131746873)
XLA Ops:
  4.9 3.2 collective-permute-start
  10.9 5.6 %fusion = (bf16[4,640,640]{2,1,0:T(8,128)(2,1)}, bf16[4,640,640]{2,1,0:T(8,128)(2,1)S(1)}) fusion(f32[4,640,640]{2,1,0:T(8,128)} %param.10), kind=kLoop, calls=%fused_computation.6 | loop fusion | flops 6553600 | bytes 13107200 | tf_op jit(solution)/shard_map/convert_element_type | solution.py:22
  16.5 4.0 pad_maximum_fusion.ext
  20.5 21.0 %shard_map.95 = f32[16,64,640]{2,1,0:T(8,128)} custom-call(s32[1]{0:T(128)} %copy.135.counts, s32[16,7]{1,0:T(8,128)S(1)} %copy.56.near, s32[16,7]{1,0:T(8,128)S(1)} %copy.57.kinds, f32[22,64,640]{2,1,0:T(8,128)} %pad_maximum_fusion.ext, bf16[4,640,640]{2,1,0:T(8,128)(2,1)S(1)} %get-tuple-element.3.top_ref, bf16[4,640,640]{2,1,0:T(8,128)(2,1)} %get-tuple-element.2.low_ref), custom_call_target="tpu_custom_call" | custom-call | flops 10066329600 | bytes 12779520 | tf_op jit(solution)/shard_map/pallas_call | solution.py:56
  41.5 2.5 slice.148
  47.8 7.3 %collective-permute-start.2 = (f32[3,32,640]{2,1,0:T(8,128)S(1)}, f32[3,32,640]{2,1,0:T(8,128)S(1)}, u32[]{:S(2)}, u32[]{:S(2)}) collective-permute-start(f32[3,32,640]{2,1,0:T(8,128)S(1)} %gather_fusion.2), channel_id=1, source_target_pairs={{0,4},{4,8},{8,12},{12,16},{16,20},{20,24},{24,28},{1,5},{5,9},{9,... | collective-permute-start | bytes 737288 | tf_op jit(solution)/shard_map/ppermute | solution.py:17
  59.9 12.6 %shard_map.96 = f32[16,32,640]{2,1,0:T(8,128)S(1)} custom-call(s32[1]{0:T(128)} %copy.135.counts, s32[16,7]{1,0:T(8,128)S(1)} %copy.56.near, s32[16,7]{1,0:T(8,128)S(1)} %copy.57.kinds, f32[22,32,640]{2,1,0:T(8,128)S(1)} %pad_maximum_fusion.2.ext, bf16[4,640,640]{2,1,0:T(8,128)(2,1)} %copy-done, bf16[4,640,640]{2,1,0:T(8,128)(2,1)} %get-tuple-element.2.low_ref), custom_call_target="tpu_custom_call" | custom-call | flops 5033164800 | bytes 9666560 | tf_op jit(solution)/shard_map/pallas_call | solution.py:56
  72.5 35.9 %all_to_all.81 = f32[16,32,640]{2,1,0:T(8,128)} all-to-all(f32[16,32,640]{2,1,0:T(8,128)S(1)} %shard_map.96), channel_id=1, replica_groups=mesh['rows'=8,'cols'=4] {'cols'}, dimensions={0} | all-to-all | bytes 2621440 | tf_op jit(solution)/shard_map/all_to_all | solution.py:227
  108.3 63.6 %all_to_all.82 = f32[16,64,640]{2,1,0:T(8,128)} all-to-all(f32[16,64,640]{2,1,0:T(8,128)S(1)} %fusion.1), channel_id=1, replica_groups=mesh['rows'=8,'cols'=4] {'cols'}, dimensions={0} | all-to-all | bytes 5242880 | tf_op jit(solution)/shard_map/all_to_all | solution.py:227
  172.0 4.2 all-to-all-start.1
  176.2 2.2 copy.61
  184.1 51.7 %all-to-all-done.1 = f32[16,64,640]{2,1,0:T(8,128)S(1)} async-done(((f32[16,64,640]{2,1,0:T(8,128)}), f32[16,64,640]{2,1,0:T(8,128)S(1)}, u32[]{:S(2)}, u32[]{:S(2)}) %all-to-all-start.1) | async-done | bytes 2621472 | tf_op jit(solution)/shard_map/all_to_all | solution.py:227
  240.1 8.5 %fusion.9 = f32[640,640]{1,0:T(8,128)S(1)} fusion(f32[640,2560]{1,0:T(8,128)S(1)} %constant_dynamic-update-slice_fusion), kind=kOutput, calls=%fused_computation.70 | convolution fusion | flops 6291456000 | bytes 8192000 | tf_op jit(solution)/shard_map/dot_general | solution.py:237
  249.2 20.5 %all_to_all.83 = f32[8,4,7680]{2,1,0:T(4,128)S(1)} all-to-all(f32[8,4,7680]{2,1,0:T(4,128)S(1)} %reshape.111), channel_id=1, replica_groups=mesh['rows'=8,'cols'=4] {'rows'}, dimensions={0} | all-to-all | bytes 1966080 | tf_op jit(solution)/shard_map/all_to_all | solution.py:197
  269.9 8.5 %all_to_all.84 = f32[4,1,7680]{2,1,0:T(1,128)S(1)} all-to-all(f32[4,1,7680]{2,1,0:T(1,128)S(1)} %all_to_all.59), channel_id=1, replica_groups=mesh['rows'=8,'cols'=4] {'cols'}, dimensions={0} | all-to-all | bytes 245760 | tf_op jit(solution)/shard_map/all_to_all | solution.py:198
  278.6 8.3 %all_to_all.85 = f32[4,1,7680]{2,1,0:T(1,128)S(1)} all-to-all(f32[4,1,7680]{2,1,0:T(1,128)S(1)} %broadcast_in_dim.4), channel_id=1, replica_groups=mesh['rows'=8,'cols'=4] {'cols'}, dimensions={0} | all-to-all | bytes 245760 | tf_op jit(solution)/shard_map/all_to_all | solution.py:199
  287.1 17.1 %all_to_all.86 = f32[8,4,7680]{2,1,0:T(4,128)S(1)} all-to-all(f32[8,4,7680]{2,1,0:T(4,128)S(1)} %broadcast_in_dim.5), channel_id=1, replica_groups=mesh['rows'=8,'cols'=4] {'rows'}, dimensions={0} | all-to-all | bytes 1966080 | tf_op jit(solution)/shard_map/all_to_all | solution.py:200
  319.3 79.9 %shard_map.97 = f32[640,256]{1,0:T(8,128)S(1)} custom-call(f32[640,640]{1,0:T(8,128)S(1)} %slice_dynamic-update-slice_fusion.1.gram_ref, f32[2,384,256]{2,1,0:T(8,128)S(1)} %copy-done.1), custom_call_target="tpu_custom_call" | custom-call | tf_op jit(solution)/shard_map/pallas_call | solution.py:177
  399.3 6.3 %fusion.2 = f32[128,2560]{1,0:T(8,128)} fusion(f32[640,2560]{1,0:T(8,128)} %copy-done.3, f32[640,256]{1,0:T(8,128)S(1)} %shard_map.97), kind=kOutput, calls=%fused_computation.13 | convolution fusion | flops 1258291200 | bytes 8192000 | tf_op jit(solution)/shard_map/dot_general | solution.py:254
  405.5 3.5 all-to-all-start.8
  409.1 6.0 %fusion.4 = f32[128,2560]{1,0:T(8,128)} fusion(f32[640,2560]{1,0:T(8,128)} %copy-done.3, f32[640,256]{1,0:T(8,128)S(1)} %shard_map.97), kind=kOutput, calls=%fused_computation.15 | convolution fusion | flops 1258291200 | bytes 8192000 | tf_op jit(solution)/shard_map/dot_general | solution.py:254
  415.1 25.3 %all-to-all-done.8 = f32[4,32,2560]{2,1,0:T(8,128)S(1)} async-done(((f32[4,32,2560]{2,1,0:T(8,128)}), f32[4,32,2560]{2,1,0:T(8,128)S(1)}, u32[]{:S(2)}, u32[]{:S(2)}) %all-to-all-start.8) | async-done | bytes 1310752 | tf_op jit(solution)/shard_map/all_to_all | solution.py:255
  440.3 3.5 all-to-all-start.7
  445.0 29.7 %all-to-all-done.7 = f32[4,32,2560]{2,1,0:T(8,128)S(1)} async-done(((f32[4,32,2560]{2,1,0:T(8,128)}), f32[4,32,2560]{2,1,0:T(8,128)S(1)}, u32[]{:S(2)}, u32[]{:S(2)}) %all-to-all-start.7) | async-done | bytes 1310752 | tf_op jit(solution)/shard_map/all_to_all | solution.py:255
  (106 shorter events, 43.3 us)
Async XLA Ops:
  4.3 6.4 %copy-start.7 = (s32[16,7]{0,1:T(8,128)S(1)}, s32[16,7]{0,1:T(8,128)}, u32[]{:S(2)}) copy-start(s32[16,7]{0,1:T(8,128)} %param.13) | copy-start | bytes 1348
  4.3 6.5 %copy-start.8 = (s32[16,7]{0,1:T(8,128)S(1)}, s32[16,7]{0,1:T(8,128)}, u32[]{:S(2)}) copy-start(s32[16,7]{0,1:T(8,128)} %param.14) | copy-start | bytes 1348
  4.9 11.6 %collective-permute-start = (f32[3,64,640]{2,1,0:T(8,128)S(1)}, f32[3,64,640]{2,1,0:T(8,128)}, u32[]{:S(2)}, u32[]{:S(2)}) collective-permute-start(f32[3,64,640]{2,1,0:T(8,128)S(1)} %gather_fusion), channel_id=1, source_target_pairs={{0,4},{4,8},{8,12},{12,16},{16,20},{20,24},{24,28},{1,5},{5,9},{9,... | collective-permute-start | bytes 1474568 | tf_op jit(solution)/shard_map/ppermute | solution.py:17
  9.4 7.1 %collective-permute-start.1 = (f32[3,64,640]{2,1,0:T(8,128)}, f32[3,64,640]{2,1,0:T(8,128)}, u32[]{:S(2)}, u32[]{:S(2)}) collective-permute-start(f32[3,64,640]{2,1,0:T(8,128)} %gather_fusion.1), channel_id=1, source_target_pairs={{4,0},{8,4},{12,8},{16,12},{20,16},{24,20},{28,24},{5,1},{9,5},{13... | collective-permute-start | bytes 1474568 | tf_op jit(solution)/shard_map/ppermute | solution.py:17
  16.5 4.0 copy-start
  47.8 8.6 %collective-permute-start.2 = (f32[3,32,640]{2,1,0:T(8,128)S(1)}, f32[3,32,640]{2,1,0:T(8,128)S(1)}, u32[]{:S(2)}, u32[]{:S(2)}) collective-permute-start(f32[3,32,640]{2,1,0:T(8,128)S(1)} %gather_fusion.2), channel_id=1, source_target_pairs={{0,4},{4,8},{8,12},{12,16},{16,20},{20,24},{24,28},{1,5},{5,9},{9,... | collective-permute-start | bytes 737288 | tf_op jit(solution)/shard_map/ppermute | solution.py:17
  55.1 3.4 collective-permute-start.3
  172.0 63.8 %all-to-all-start.1 = ((f32[16,64,640]{2,1,0:T(8,128)}), f32[16,64,640]{2,1,0:T(8,128)S(1)}, u32[]{:S(2)}, u32[]{:S(2)}) async-start(f32[16,64,640]{2,1,0:T(8,128)} %shard_map.95), calls=%async_computation.1 | async-start | bytes 5242880 | tf_op jit(solution)/shard_map/all_to_all | solution.py:227
  178.3 2.2 copy-start.4
  235.8 2.9 copy-start.2
  238.6 1.3 copy-start.5
  240.0 8.5 %copy-start.3 = (f32[640,2560]{1,0:T(8,128)}, f32[640,2560]{1,0:T(8,128)S(1)}, u32[]{:S(2)}) copy-start(f32[640,2560]{1,0:T(8,128)S(1)} %constant_dynamic-update-slice_fusion) | copy-start | bytes 19660804
  312.3 2.8 copy-start.6
  315.1 4.2 copy-start.1
  405.5 34.8 %all-to-all-start.8 = ((f32[4,32,2560]{2,1,0:T(8,128)}), f32[4,32,2560]{2,1,0:T(8,128)S(1)}, u32[]{:S(2)}, u32[]{:S(2)}) async-start(f32[4,32,2560]{2,1,0:T(8,128)} %bitcast.24), calls=%async_computation.8 | async-start | bytes 2621440 | tf_op jit(solution)/shard_map/all_to_all | solution.py:255
  440.3 34.4 %all-to-all-start.7 = ((f32[4,32,2560]{2,1,0:T(8,128)}), f32[4,32,2560]{2,1,0:T(8,128)S(1)}, u32[]{:S(2)}, u32[]{:S(2)}) async-start(f32[4,32,2560]{2,1,0:T(8,128)} %bitcast.22), calls=%async_computation.7 | async-start | bytes 2621440 | tf_op jit(solution)/shard_map/all_to_all | solution.py:255
